TPU v7x, 32 devices: a whole 2x2x4 slice. The times are simulated.
32 devices in a mesh: dp: 8 (over z, y), row: 2 (over core), col: 2 (over x).
Axes of the slice: x: 2, y: 2, z: 4, core: 2. Of those that a mesh axis runs over, the one named last changes fastest.
Arguments:
- block_input: bfloat16 [4096, 2560], P(('dp', 'col')), may hold values from -6 to 6
- cotangent: bfloat16 [4096, 2560], P(('dp', 'col'), 'row'), may hold values from -6 to 6
- seq_lengths: int32 [32], replicated, may hold values from 16 to 128, as said below
- seq_owner: int32 [32], replicated, may hold values from 0 to 15, as said below
- norm_gain: bfloat16 [2560], P('row'), may hold values from 0.5 to 1.5
- proj_zx: bfloat16 [2560, 2, 5120], P('row', None, 'col'), may hold values from -0.125 to 0.125
- proj_bc: bfloat16 [2560, 256], P('row'), may hold values from -0.125 to 0.125
- proj_dt: bfloat16 [2560, 80], P('row', 'col'), may hold values from -0.125 to 0.125
- proj_out: bfloat16 [5120, 2560], P('col', 'row'), may hold values from -0.078125 to 0.078125
- inner_kernel: float32 [4, 5120], P(None, 'col'), may hold values from -3 to 3
- inner_offset: float32 [5120], P('col'), may hold values from -1.5 to 1.5
- shared_kernel: float32 [4, 256], replicated, may hold values from -3 to 3
- shared_offset: float32 [256], replicated, may hold values from -1.5 to 1.5
- decay_log: float32 [80], P('col'), may hold values from 0 to 2.77
- step_bias: float32 [80], P('col'), may hold values from -6 to -2
- skip_gain: float32 [80], P('col'), may hold values from 0.5 to 1.5
- output_gain: bfloat16 [5120], P('col'), may hold values from 0.5 to 1.5
Outputs:
- block_output: bfloat16 [4096, 2560], P(('dp', 'col'), 'row')
- input_grad: float32 [4096, 2560], P(('dp', 'col'), 'row')
- grad_norm: float32 [2560], P('row')
- grad_inproj: float32 [2560, 2, 5120], P('row', None, 'col')
- grad_shared: float32 [2560, 256], P('row')
- grad_steps: float32 [2560, 80], P('row', 'col')
- grad_outproj: float32 [5120, 2560], P('col', 'row')
- grad_kernel: float32 [4, 5120], P(None, 'col')
- grad_offset: float32 [5120], P('col')
- grad_skernel: float32 [4, 256], replicated
- grad_soffset: float32 [256], replicated
- grad_decay: float32 [80], P('col')
- grad_stepbias: float32 [80], P('col')
- grad_skip: float32 [80], P('col')
- grad_ogain: float32 [5120], P('col')
Inputs may be any that keep to these rules, and one draw needn't show every extreme that they name: `seq_lengths`: the lengths of the 2 sequences of one bucket sum to at most 256; in every draw some bucket holds 2 sequences of exactly 128 rows, so that its sum is 256. `seq_owner`: every bucket owns exactly 2 sequences.
All inputs are finite; a program needn't handle non-finite values.
Results may differ from a plain program's by a relative error of at most 0.0079.
The roundings to bfloat16 on the way count: a program that leaves them out, or rounds other values in their place, can miss the bound.
Values may be sent and summed in bfloat16 or wider, within the bound.
A program may use at most 256 MiB of HBM per device.

v0:
```python
import jax
import jax.numpy as jnp
from jax import lax
from jax.sharding import PartitionSpec as P

D = 2560
DI = 5120
CAP = 256
EPSILON = 1e-05
PRECISE = lax.Precision.HIGHEST


def layout(seq_lengths, seq_owner, bucket, capacity):
    owned = seq_owner == bucket
    owned_len = jnp.where(owned, seq_lengths, 0)
    order = jnp.arange(seq_lengths.shape[0], dtype=jnp.int32)
    starts = jnp.sum(jnp.where(order[None, :] < order[:, None], owned_len[None, :], 0), axis=1)
    places = jnp.arange(capacity, dtype=jnp.int32)[:, None]
    ends = starts + seq_lengths
    inside = owned[None, :] & (places >= starts[None, :]) & (places < ends[None, :])
    live_rows = jnp.any(inside, axis=1)
    seq_index = jnp.arange(seq_lengths.shape[0], dtype=jnp.int32)
    seq_ids = jnp.sum(jnp.where(inside, seq_index[None, :], 0), axis=1)
    seq_ids = jnp.where(live_rows, seq_ids, -1)
    return (seq_ids, live_rows.astype(jnp.float32))


def convolve(channels, kernel, offset, seq_ids, live_rows):
    tap_count = kernel.shape[0]
    summed_in = offset[None, :] + kernel[tap_count - 1][None, :] * channels
    for lag_steps in range(1, tap_count):
        lagged = jnp.concatenate(
            [jnp.zeros((lag_steps, channels.shape[1]), jnp.float32), channels[:-lag_steps]], axis=0
        )
        prior_ids = jnp.concatenate([jnp.full((lag_steps,), -1, jnp.int32), seq_ids[:-lag_steps]])
        same_seq = jnp.where((prior_ids == seq_ids) & (live_rows > 0), 1.0, 0.0).astype(jnp.float32)
        summed_in = (
            summed_in + kernel[tap_count - 1 - lag_steps][None, :] * lagged * same_seq[:, None]
        )
    return summed_in


def mix_bucket(values, bmat, cmat, sizes, rates, skip_gain, ids, live):
    rows_all, head_count, head_dim = values.shape
    lower = jnp.arange(rows_all)[:, None] >= jnp.arange(rows_all)[None, :]
    cumulated = jnp.dot(lower.astype(jnp.float32), rates, precision=PRECISE)
    pair_live = (ids[:, None] == ids[None, :]) & (live[:, None] > 0) & (live[None, :] > 0) & lower
    scores = jnp.dot(cmat, bmat.T, precision=PRECISE)
    gap = jnp.where(pair_live[:, :, None], cumulated[:, None, :] - cumulated[None, :, :], 0.0)
    weights = (
        jnp.exp(gap) * (pair_live.astype(jnp.float32) * scores)[:, :, None] * sizes[None, :, :]
    )
    within = jnp.einsum("tsh,shp->thp", weights, values, precision=PRECISE)
    mixed_out = (within + skip_gain[None, :, None] * values) * live[:, None, None]
    return mixed_out.reshape(rows_all, head_count * head_dim)


def sum_rows_over_dp(part, shared_cols=0):
    piece = lax.psum_scatter(part.astype(jnp.bfloat16), "dp", scatter_dimension=0, tiled=True)
    if shared_cols:
        own = piece.shape[1] - shared_cols
        tail = lax.psum(piece[:, own:].astype(jnp.float32), "col").astype(jnp.bfloat16)
        piece = jnp.concatenate([piece[:, :own], tail], axis=1)
    return lax.all_gather(piece, "dp", axis=0, tiled=True)


def mixer_local(
    conv_in,
    narrow_in,
    inner_kernel,
    inner_offset,
    shared_kernel,
    shared_offset,
    decay_log,
    step_bias,
    skip_gain,
    seq_ids,
    live_rows,
):
    inner_size = inner_kernel.shape[1]
    state_size = shared_kernel.shape[1] // 2
    head_count = decay_log.shape[0]
    shared_in = narrow_in[:, : 2 * state_size]
    step_raw = narrow_in[:, 2 * state_size :]
    mixed_x = jax.nn.silu(convolve(conv_in, inner_kernel, inner_offset, seq_ids, live_rows))
    mixed_bc = jax.nn.silu(convolve(shared_in, shared_kernel, shared_offset, seq_ids, live_rows))
    step_sizes = jax.nn.softplus(step_raw + step_bias[None, :])
    decay_rate = step_sizes * (-jnp.exp(decay_log))[None, :]
    values = mixed_x.reshape(mixed_x.shape[0], head_count, inner_size // head_count)
    return mix_bucket(
        values,
        mixed_bc[:, :state_size],
        mixed_bc[:, state_size:],
        step_sizes,
        decay_rate,
        skip_gain,
        seq_ids,
        live_rows,
    )


def per_device(
    block_input,
    cotangent,
    seq_lengths,
    seq_owner,
    norm_gain,
    proj_zx,
    proj_bc,
    proj_dt,
    proj_out,
    inner_kernel,
    inner_offset,
    shared_kernel,
    shared_offset,
    decay_log,
    step_bias,
    skip_gain,
    output_gain,
):
    row_count = lax.axis_size("row")
    col_count = lax.axis_size("col")
    row_index = lax.axis_index("row")
    col_index = lax.axis_index("col")
    data_index = lax.axis_index("dp")
    width_part = norm_gain.shape[0]
    inner_size = proj_zx.shape[2]
    state_size = proj_bc.shape[1] // 2
    tap_count = inner_kernel.shape[0]
    capacity = CAP
    bucket = data_index * row_count + row_index
    seq_ids, live_rows = layout(seq_lengths, seq_owner, bucket, capacity)
    rscale = lax.rsqrt(
        jnp.mean(jnp.square(block_input.astype(jnp.float32)), axis=1, keepdims=True) + EPSILON
    )
    own_cols = lax.dynamic_slice_in_dim(block_input, row_index * width_part, width_part, 1).astype(
        jnp.float32
    )
    normalized = own_cols * rscale
    gain_f = norm_gain.astype(jnp.float32)
    normed = (normalized * gain_f[None, :]).astype(jnp.bfloat16)
    normed_all = lax.all_gather(normed, "col", axis=0, tiled=True)
    weight_zx = proj_zx.reshape(width_part, 2 * inner_size)
    weight_narrow = jnp.concatenate([proj_bc, proj_dt], axis=1)
    zx_in = lax.psum_scatter(
        jnp.dot(normed_all, weight_zx, preferred_element_type=jnp.float32),
        "row",
        scatter_dimension=0,
        tiled=True,
    )
    narrow_in = lax.psum_scatter(
        jnp.dot(normed_all, weight_narrow, preferred_element_type=jnp.float32),
        "row",
        scatter_dimension=0,
        tiled=True,
    )
    gate_in = zx_in[:, :inner_size]
    conv_in = zx_in[:, inner_size:]

    def local_piece(*operands):
        return mixer_local(*operands, seq_ids, live_rows)

    ssm_rows, pull_back = jax.vjp(
        local_piece,
        conv_in,
        narrow_in,
        inner_kernel,
        inner_offset,
        shared_kernel,
        shared_offset,
        decay_log,
        step_bias,
        skip_gain,
    )
    gated_rows, gate_back = jax.vjp(
        lambda ssm_value, gate_value: ssm_value * jax.nn.silu(gate_value), ssm_rows, gate_in
    )
    square_sum = lax.psum(jnp.sum(gated_rows * gated_rows, axis=1), "col")
    rnorm = lax.rsqrt(square_sum / DI + EPSILON)[:, None]
    out_gain = output_gain.astype(jnp.float32)
    branch = (gated_rows * rnorm * out_gain[None, :]).astype(jnp.bfloat16)
    branch_all = lax.all_gather(branch, "row", axis=0, tiled=True)
    row_piece = branch_all
    branch_out = lax.psum_scatter(
        jnp.dot(row_piece, proj_out, preferred_element_type=jnp.float32),
        "col",
        scatter_dimension=0,
        tiled=True,
    )
    block_output = (own_cols + branch_out).astype(jnp.bfloat16)
    cot_all = lax.all_gather(cotangent, "col", axis=0, tiled=True)
    row_piece = cot_all
    branch_grad = lax.psum_scatter(
        lax.dot_general(
            row_piece, proj_out, (((1,), (1,)), ((), ())), preferred_element_type=jnp.float32
        ),
        "row",
        scatter_dimension=0,
        tiled=True,
    )
    outproj_part = lax.dot_general(
        branch_all, cot_all, (((0,), (0,)), ((), ())), preferred_element_type=jnp.float32
    )
    outproj_total = sum_rows_over_dp(outproj_part).astype(jnp.float32)
    scaled_grad = branch_grad * out_gain[None, :]
    cross_sum = lax.psum(jnp.sum(scaled_grad * gated_rows, axis=1), "col")
    gated_grad = rnorm * scaled_grad - gated_rows * rnorm**3 * (cross_sum / DI)[:, None]
    ogain_part = jnp.sum(branch_grad * gated_rows * rnorm, axis=0)
    ssm_grad, gate_grad = gate_back(gated_grad)
    gate_all = lax.all_gather(gate_grad.astype(jnp.bfloat16), "row", axis=0, tiled=True)
    gate_total = sum_rows_over_dp(
        lax.dot_general(
            normed_all, gate_all, (((0,), (0,)), ((), ())), preferred_element_type=jnp.float32
        )
    )
    local_grads = pull_back(ssm_grad)
    inner_all = lax.all_gather(local_grads[0].astype(jnp.bfloat16), "row", axis=0, tiled=True)
    narrow_all = lax.all_gather(local_grads[1].astype(jnp.bfloat16), "row", axis=0, tiled=True)
    normed_grad = lax.psum_scatter(
        lax.dot_general(
            jnp.concatenate([gate_all, inner_all], axis=1),
            weight_zx,
            (((1,), (1,)), ((), ())),
            preferred_element_type=jnp.float32,
        )
        + lax.dot_general(
            narrow_all, weight_narrow, (((1,), (1,)), ((), ())), preferred_element_type=jnp.float32
        ),
        "col",
        scatter_dimension=0,
        tiled=True,
    )
    inner_total = sum_rows_over_dp(
        lax.dot_general(
            normed_all, inner_all, (((0,), (0,)), ((), ())), preferred_element_type=jnp.float32
        )
    )
    narrow_part = lax.dot_general(
        normed_all, narrow_all, (((0,), (0,)), ((), ())), preferred_element_type=jnp.float32
    )
    narrow_total = sum_rows_over_dp(
        jnp.concatenate([narrow_part[:, 2 * state_size :], narrow_part[:, : 2 * state_size]], 1),
        2 * state_size,
    ).astype(jnp.float32)
    head_count = decay_log.shape[0]
    steps_total = narrow_total[:, :head_count]
    shared_total = narrow_total[:, head_count:]
    inproj_total = jnp.stack([gate_total, inner_total], axis=1).astype(jnp.float32)
    scaled_in = normed_grad * gain_f[None, :]
    norm_part = jnp.sum(normed_grad * normalized, axis=0)
    row_stat = lax.psum(jnp.sum(scaled_in * normalized, axis=1), "row")
    input_grad = cotangent.astype(jnp.float32) + rscale * (
        scaled_in - normalized * (row_stat / D)[:, None]
    )
    row_hot = (jnp.arange(row_count) == row_index).astype(jnp.float32)
    col_hot = (jnp.arange(col_count) == col_index).astype(jnp.float32)
    gain_slot = row_hot[:, None] * norm_part[None, :]
    head_stack = jnp.stack([local_grads[6], local_grads[7], local_grads[8]], axis=0)
    head_slot = col_hot[None, :, None] * head_stack[:, None, :]
    chan_stack = jnp.concatenate(
        [local_grads[2], local_grads[3][None, :], ogain_part[None, :]], axis=0
    )
    chan_slot = col_hot[None, :, None] * chan_stack[:, None, :]
    shared_stack = jnp.concatenate([local_grads[4], local_grads[5][None, :]], axis=0)
    summed = lax.psum((gain_slot, head_slot, chan_slot, shared_stack), ("dp", "row", "col"))
    gain_total = lax.dynamic_index_in_dim(summed[0], row_index, 0, keepdims=False)
    head_total = lax.dynamic_index_in_dim(summed[1], col_index, 1, keepdims=False)
    chan_total = lax.dynamic_index_in_dim(summed[2], col_index, 1, keepdims=False)
    stack_total = summed[3]
    return (
        block_output,
        input_grad,
        gain_total,
        inproj_total,
        shared_total,
        steps_total,
        outproj_total,
        chan_total[:tap_count],
        chan_total[tap_count],
        stack_total[:tap_count],
        stack_total[tap_count],
        head_total[0],
        head_total[1],
        head_total[2],
        chan_total[tap_count + 1],
    )


def solution(mesh):
    return jax.shard_map(
        per_device,
        mesh=mesh,
        in_specs=(
            P(("dp", "col"), None),
            P(("dp", "col"), "row"),
            P(),
            P(),
            P("row"),
            P("row", None, "col"),
            P("row", None),
            P("row", "col"),
            P("col", "row"),
            P(None, "col"),
            P("col"),
            P(),
            P(),
            P("col"),
            P("col"),
            P("col"),
            P("col"),
        ),
        out_specs=(
            P(("dp", "col"), "row"),
            P(("dp", "col"), "row"),
            P("row"),
            P("row", None, "col"),
            P("row", None),
            P("row", "col"),
            P("col", "row"),
            P(None, "col"),
            P("col"),
            P(),
            P(),
            P("col"),
            P("col"),
            P("col"),
            P("col"),
        ),
        check_vma=False,
    )
```

profile of v0, /device:TPU:0, one launch (start us, length us, event | category | flops | bytes accessed | tf_op | source)
XLA Modules:
  0.0 1226.2 jit_solution(14746132511163028913)
XLA Ops:
  12.6 12.3 %copy.74 = bf16[160,8,2,2560]{3,1,2,0:T(8,128)(2,1)} copy(bf16[160,8,2,2560]{3,2,1,0:T(2,128)(2,1)} %bitcast.83) | data formatting | bytes 26214400
  25.1 13.7 %all-gather.9.cloned.1.call-done = bf16[512,1280]{1,0:T(8,128)(2,1)} async-done(((bf16[256,1280]{1,0:T(8,128)(2,1)}), bf16[512,1280]{1,0:T(8,128)(2,1)}) %all-gather.9.cloned.1.call-update) | async-done | bytes 1310736 | tf_op jit(solution)/shard_map/all_gather | solution.py:142
  41.8 12.3 %fusion.106 = f32[512,5120]{1,0:T(8,128)} fusion(bf16[512,1280]{1,0:T(8,128)(2,1)S(1)} %copy-done.17, bf16[1280,5120]{1,0:T(8,128)(2,1)} %bitcast.84), kind=kOutput, calls=%fused_computation.194 | convolution fusion | flops 6710886400 | bytes 24903680 | tf_op jit(solution)/shard_map/dot_general | solution.py:146
  54.2 10.5 all-gather.13.cloned.1.call-done
  64.7 9.2 fusion.108
  83.8 14.8 %reduce-scatter.12.cloned.1.call-done = f32[256,5120]{1,0:T(8,128)} async-done(((f32[512,5120]{1,0:T(8,128)}), f32[256,5120]{1,0:T(8,128)}) %reduce-scatter.12.cloned.1.call-update) | async-done | bytes 5242896 | tf_op jit(solution)/shard_map/reduce_scatter | solution.py:145
  110.1 15.6 %fusion.33 = f32[256,40,64]{0,2,1:T(8,128)} fusion(f32[256,40,64]{0,2,1:T(8,128)} %bitcast.88, f32[256,40]{0,1:T(8,128)S(1)} %compare_select_fusion.2, f32[256,256]{1,0:T(8,128)} %convolution_select_fusion, f32[256,40]{0,1:T(8,128)S(1)} %fusion.64, pred[256,256]{1,0:T(8,128)(4,1)S(1)} %fusion.65, f32[256]{0:T(256)S(1)} %get-tuple-element.145, ...), kind=kOutput, calls=%fused_computation.49 | convolution fusion | flops 2025717760 | bytes 5653664 | tf_op jit(solution)/shard_map/jvp(tsh,shp->thp)/dot_general | solution.py:53
  131.9 4.9 psum.56
  140.1 5.2 psum.57
  145.3 6.7 multiply_reduce_fusion.1
  154.2 11.6 bitcast_add_fusion
  182.7 18.6 %fusion.8 = (f32[256,40]{0,1:T(8,128)}, f32[256,40]{0,1:T(8,128)}, f32[256,40]{0,1:T(8,128)}, f32[256,256]{1,0:T(8,128)S(1)}) fusion(f32[256,40]{0,1:T(8,128)} %copy-done.31, f32[256,256]{1,0:T(8,128)} %convolution_select_fusion, f32[256,40]{0,1:T(8,128)} %copy-done.66, pred[256,256]{1,0:T(8,128)(4,1)S(1)} %fusion.65, f32[256,40,64]{0,2,1:T(8,128)S(1)} %bitcast.89, ...), kind=kOutput, calls=%fused_computation.15 | convolution fusion | flops 2047903744 | bytes 6038528 | tf_op jit(solution)/shard_map/transpose(jvp(tsh,shp->thp))/dot_general | solution.py:53
  210.6 7.3 convolution_convert_fusion.1
  218.0 7.6 convolution_convert_fusion.2
  226.9 8.0 convolution_convert_fusion
  236.7 55.0 %reduce-scatter.28.cloned.1.call-done = bf16[160,296]{1,0:T(8,128)(2,1)} async-done(((bf16[1280,296]{1,0:T(8,128)(2,1)}), bf16[160,296]{1,0:T(8,128)(2,1)}) %reduce-scatter.28.cloned.1.call-update) | async-done | bytes 94736
  293.5 13.9 %fusion.9 = f32[512,1280]{1,0:T(8,128)} fusion(bf16[1280,5120]{1,0:T(8,128)(2,1)} %bitcast.85, bf16[512,2560]{1,0:T(8,128)(2,1)} %all-gather.17.cloned.1.call-done, bf16[512,2560]{1,0:T(8,128)(2,1)} %all-gather.15.cloned.1.call-done), kind=kOutput, calls=%fused_computation.16 | convolution fusion | flops 6721372160 | bytes 20971520 | tf_op jit(solution)/shard_map/dot_general | solution.py:220
  307.4 4.1 convolution_add_fusion
  313.2 7.9 fusion.107
  321.2 95.2 %reduce-scatter.24.cloned.1.call-done = bf16[160,2560]{1,0:T(8,128)(2,1)} async-done(((bf16[1280,2560]{1,0:T(8,128)(2,1)}), bf16[160,2560]{1,0:T(8,128)(2,1)}) %reduce-scatter.24.cloned.1.call-update) | async-done | bytes 819216 | tf_op jit(solution)/shard_map/reduce_scatter | solution.py:59
  416.4 124.8 %reduce-scatter.22.cloned.1.call-done = bf16[160,2560]{1,0:T(8,128)(2,1)} async-done(((bf16[1280,2560]{1,0:T(8,128)(2,1)}), bf16[160,2560]{1,0:T(8,128)(2,1)}) %reduce-scatter.22.cloned.1.call-update) | async-done | bytes 819216 | tf_op jit(solution)/shard_map/reduce_scatter | solution.py:59
  541.3 124.2 %reduce-scatter.26.cloned.1.call-done = bf16[320,1280]{1,0:T(8,128)(2,1)} async-done(((bf16[2560,1280]{1,0:T(8,128)(2,1)}), bf16[320,1280]{1,0:T(8,128)(2,1)}) %reduce-scatter.26.cloned.1.call-update) | async-done | bytes 819216 | tf_op jit(solution)/shard_map/reduce_scatter | solution.py:59
  665.9 127.6 %all-reduce.32.cloned.1.call-done = f32[6,2,2560]{2,0,1:T(8,128)} async-done(((f32[6,2,2560]{2,0,1:T(8,128)}), f32[6,2,2560]{2,0,1:T(8,128)}) %all-reduce.32.cloned.1.call-update) | async-done | bytes 122896 | tf_op jit(solution)/shard_map/psum | solution.py:265
  796.7 23.0 %all-reduce.30.cloned.1.call-done = bf16[160,256]{0,1:T(8,128)(2,1)} async-done(((bf16[160,256]{0,1:T(8,128)(2,1)}), bf16[160,256]{0,1:T(8,128)(2,1)}) %all-reduce.30.cloned.1.call-update) | async-done | bytes 81936 | tf_op jit(solution)/shard_map/psum | solution.py:62
  820.8 33.0 %all_gather.38 = bf16[1280,296]{1,0:T(8,128)(2,1)S(1)} all-gather(bf16[160,296]{1,0:T(8,128)(2,1)S(1)} %copy.67), channel_id=1, replica_groups=mesh['dp'=8,'row'=2,'col'=2] {'dp'}, dimensions={0}, use_global_device_ids=true | all-gather | bytes 852480 | tf_op jit(solution)/shard_map/all_gather | solution.py:64
  862.1 40.3 %all-reduce.26 = (f32[2,1280]{1,0:T(2,128)S(1)}, f32[5,256]{1,0:T(8,128)S(1)}, f32[3,2,40]{2,1,0:T(2,128)S(1)}) all-reduce(f32[2,1280]{1,0:T(2,128)S(1)} %broadcast_multiply_fusion.7, f32[5,256]{1,0:T(8,128)S(1)} %pad_maximum_fusion.6, ...), channel_id=1, replica_groups=mesh['dp'=8,'row'=2,'col'=2] {'dp','row','col'}, use_global_device_ids=true, to_apply=%region_20.21 | all-reduce | flops 4080 | bytes 32640 | tf_op jit(solution)/shard_map/psum | solution.py:265
  910.2 94.8 %all-gather.21.cloned.1.call-done = bf16[1280,2560]{1,0:T(8,128)(2,1)} async-done(((bf16[160,2560]{1,0:T(8,128)(2,1)}), bf16[1280,2560]{1,0:T(8,128)(2,1)}) %all-gather.21.cloned.1.call-update) | async-done | bytes 6553616 | tf_op jit(solution)/shard_map/all_gather | solution.py:64
  1005.0 102.7 %all-gather.19.cloned.1.call-done = bf16[1280,2560]{1,0:T(8,128)(2,1)} async-done(((bf16[160,2560]{1,0:T(8,128)(2,1)}), bf16[1280,2560]{1,0:T(8,128)(2,1)}) %all-gather.19.cloned.1.call-update) | async-done | bytes 6553616 | tf_op jit(solution)/shard_map/all_gather | solution.py:64
  1107.7 14.4 %maximum_convert_fusion = f32[1280,2,2560]{2,0,1:T(8,128)} fusion(bf16[1280,1,2560]{2,0,1:T(8,128)(2,1)} %bitcast.86, bf16[1280,1,2560]{2,0,1:T(8,128)(2,1)} %bitcast.87), kind=kLoop, calls=%fused_computation | loop fusion | flops 13107200 | bytes 39321600 | tf_op jit(solution)/shard_map/convert_element_type | solution.py:248
  1122.1 43.6 %copy.68 = f32[1280,2,2560]{2,1,0:T(2,128)} copy(f32[1280,2,2560]{2,0,1:T(8,128)} %maximum_convert_fusion) | data formatting | bytes 52428800
  1165.7 44.9 %all-gather.23.cloned.1.call-done = bf16[2560,1280]{1,0:T(8,128)(2,1)} async-done(((bf16[320,1280]{1,0:T(8,128)(2,1)}), bf16[2560,1280]{1,0:T(8,128)(2,1)}) %all-gather.23.cloned.1.call-update) | async-done | bytes 6553616 | tf_op jit(solution)/shard_map/all_gather | solution.py:64
  1210.6 8.8 convert_element_type.112
  (283 shorter events, 94.5 us)
Async XLA Ops:
  7.2 31.7 %all-gather.9.cloned.1.call-start = ((), (), s32[]{:S(2)}) async-start(), calls=%async_computation.9 | async-start | bytes 1966080 | tf_op jit(solution)/shard_map/all_gather | solution.py:142
  11.8 52.9 %all-gather.13.cloned.1.call-start = ((), (), s32[]{:S(2)}) async-start(), calls=%async_computation.14 | async-start | bytes 1966080 | tf_op jit(solution)/shard_map/all_gather | solution.py:191
  12.5 63.1 %reduce-scatter.14.cloned.1.call-start = ((), (), s32[]{:S(2)}) async-start(), calls=%async_computation.11 | async-start | bytes 909312 | tf_op jit(solution)/shard_map/reduce_scatter | solution.py:151
  12.6 26.3 %copy-start.20 = (bf16[1280,256]{1,0:T(8,128)(2,1)S(1)}, bf16[1280,256]{1,0:T(8,128)(2,1)}, u32[]{:S(2)}) copy-start(bf16[1280,256]{1,0:T(8,128)(2,1)} %param.23) | copy-start | bytes 1966084
  25.1 29.0 %copy-start.15 = (bf16[1280,40]{1,0:T(8,128)(2,1)}, bf16[1280,40]{1,0:T(8,128)(2,1)S(1)}, u32[]{:S(2)}) copy-start(bf16[1280,40]{1,0:T(8,128)(2,1)S(1)} %copy.61) | copy-start | bytes 307204
  41.8 56.8 %reduce-scatter.12.cloned.1.call-start = ((), (), s32[]{:S(2)}) async-start(), calls=%async_computation.10 | async-start | bytes 15728640 | tf_op jit(solution)/shard_map/reduce_scatter | solution.py:145
  54.2 82.6 %reduce-scatter.18.cloned.1.call-start = ((), (), s32[]{:S(2)}) async-start(), calls=%async_computation.15 | async-start | bytes 7864320 | tf_op jit(solution)/shard_map/reduce_scatter | solution.py:193
  74.0 136.6 %all-gather.17.cloned.1.call-start = ((), (), s32[]{:S(2)}) async-start(), calls=%async_computation.17 | async-start | bytes 3932160 | tf_op jit(solution)/shard_map/all_gather | solution.py:217
  75.1 25.6 %copy-start.65 = (f32[40]{0:T(128)}, f32[40]{0:T(128)S(1)}, u32[]{:S(2)}) copy-start(f32[40]{0:T(128)S(1)} %exponential_negate_fusion) | copy-start | bytes 484
  75.1 79.1 %copy-start.53 = (f32[256]{0:T(256)}, f32[256]{0:T(256)S(1)}, u32[]{:S(2)}) copy-start(f32[256]{0:T(256)S(1)} %get-tuple-element.145) | copy-start | bytes 3076
  75.2 94.0 %copy-start.37 = (f32[256]{0:T(256)}, f32[256]{0:T(256)S(1)}, u32[]{:S(2)}) copy-start(f32[256]{0:T(256)S(1)} %get-tuple-element.142) | copy-start | bytes 3076
  75.2 98.1 %copy-start.33 = (f32[256]{0:T(256)}, f32[256]{0:T(256)S(1)}, u32[]{:S(2)}) copy-start(f32[256]{0:T(256)S(1)} %get-tuple-element.140) | copy-start | bytes 3076
  75.2 98.1 %copy-start.35 = (f32[256]{0:T(256)}, f32[256]{0:T(256)S(1)}, u32[]{:S(2)}) copy-start(f32[256]{0:T(256)S(1)} %get-tuple-element.141) | copy-start | bytes 3076
  79.6 74.6 %copy-start.31 = (f32[256,40]{0,1:T(8,128)}, f32[256,40]{0,1:T(8,128)S(1)}, u32[]{:S(2)}) copy-start(f32[256,40]{0,1:T(8,128)S(1)} %compare_select_fusion.2) | copy-start | bytes 122884
  79.9 74.4 %copy-start.66 = (f32[256,40]{0,1:T(8,128)}, f32[256,40]{0,1:T(8,128)S(1)}, u32[]{:S(2)}) copy-start(f32[256,40]{0,1:T(8,128)S(1)} %fusion.64) | copy-start | bytes 122884
  180.9 37.0 %all-gather.15.cloned.1.call-start = ((), (), s32[]{:S(2)}) async-start(), calls=%async_computation.16 | async-start | bytes 3932160 | tf_op jit(solution)/shard_map/all_gather | solution.py:210
  181.7 44.2 %all-gather.11.cloned.1.call-start = ((), (), s32[]{:S(2)}) async-start(), calls=%async_computation.12 | async-start | bytes 3932160 | tf_op jit(solution)/shard_map/all_gather | solution.py:182
  202.0 89.6 %reduce-scatter.28.cloned.1.call-start = ((), (), s32[]{:S(2)}) async-start(), calls=%async_computation.27 | async-start | bytes 1105920
  210.5 205.8 %reduce-scatter.24.cloned.1.call-start = ((), (), s32[]{:S(2)}) async-start(), calls=%async_computation.21 | async-start | bytes 7372800 | tf_op jit(solution)/shard_map/reduce_scatter | solution.py:59
  217.9 323.3 %reduce-scatter.22.cloned.1.call-start = ((), (), s32[]{:S(2)}) async-start(), calls=%async_computation.19 | async-start | bytes 7372800 | tf_op jit(solution)/shard_map/reduce_scatter | solution.py:59
  225.6 439.9 %reduce-scatter.26.cloned.1.call-start = ((), (), s32[]{:S(2)}) async-start(), calls=%async_computation.24 | async-start | bytes 7372800 | tf_op jit(solution)/shard_map/reduce_scatter | solution.py:59
  235.0 558.5 %all-reduce.32.cloned.1.call-start = ((), (), s32[]{:S(2)}) async-start(), calls=%async_computation.26 | async-start | bytes 327680 | tf_op jit(solution)/shard_map/psum | solution.py:265
  236.6 583.1 %all-reduce.30.cloned.1.call-start = ((), (), s32[]{:S(2)}) async-start(), calls=%async_computation.23 | async-start | bytes 262144 | tf_op jit(solution)/shard_map/psum | solution.py:62
  293.4 566.7 %reduce-scatter.20.cloned.1.call-start = ((), (), s32[]{:S(2)}) async-start(), calls=%async_computation.18 | async-start | bytes 3932160 | tf_op jit(solution)/shard_map/reduce_scatter | solution.py:219
  311.5 595.6 %reduce-scatter.16.cloned.1.call-start = ((), (), s32[]{:S(2)}) async-start(), calls=%async_computation.13 | async-start | bytes 3932160 | tf_op jit(solution)/shard_map/reduce_scatter | solution.py:184
  321.1 344.6 %copy-start.63 = (f32[40]{0:T(128)S(1)}, f32[40]{0:T(128)}, u32[]{:S(2)}) copy-start(f32[40]{0:T(128)} %param.30) | copy-start | bytes 484
  321.1 475.5 %slice-start.2 = ((bf16[160,296]{1,0:T(8,128)(2,1)}), bf16[160,40]{1,0:T(8,128)(2,1)S(1)}, s32[]{:S(2)}) async-start(bf16[160,296]{1,0:T(8,128)(2,1)} %reduce-scatter.28.cloned.1.call-done), calls=%async_computation.30 | async-start | bytes 81920 | tf_op jit(solution)/shard_map/slice | solution.py:63
  321.2 683.9 %all-gather.21.cloned.1.call-start = ((), (), s32[]{:S(2)}) async-start(), calls=%async_computation.22 | async-start | bytes 7372800 | tf_op jit(solution)/shard_map/all_gather | solution.py:64
  416.4 691.4 %all-gather.19.cloned.1.call-start = ((), (), s32[]{:S(2)}) async-start(), calls=%async_computation.20 | async-start | bytes 7372800 | tf_op jit(solution)/shard_map/all_gather | solution.py:64
  541.2 669.3 %all-gather.23.cloned.1.call-start = ((), (), s32[]{:S(2)}) async-start(), calls=%async_computation.25 | async-start | bytes 7372800 | tf_op jit(solution)/shard_map/all_gather | solution.py:64
  855.1 52.0 %copy-start.12 = (bf16[256,1280]{1,0:T(8,128)(2,1)S(1)}, bf16[256,1280]{1,0:T(8,128)(2,1)}, u32[]{:S(2)}) copy-start(bf16[256,1280]{1,0:T(8,128)(2,1)} %param.18) | copy-start | bytes 1966084
  860.1 47.0 %copy-start.9 = (f32[256,1280]{1,0:T(8,128)S(1)}, f32[256,1280]{1,0:T(8,128)}, u32[]{:S(2)}) copy-start(f32[256,1280]{1,0:T(8,128)} %reduce-scatter.20.cloned.1.call-done) | copy-start | bytes 3932164
  (57 other events, 365.5 us)
Sparse Core Ops, SparseCore 0:
  11.9 26.9 all-gather.8
  40.4 24.2 all-gather.12
  67.6 8.0 reduce-scatter.13
  78.4 20.1 reduce-scatter.11
  100.8 14.4 reduce-scatter.17
  181.1 12.5 all-gather.16
  195.9 12.6 all-gather.14
  210.8 12.5 all-gather.10
  227.1 64.4 reduce-scatter.27
  295.7 120.6 reduce-scatter.23
  420.4 120.7 reduce-scatter.21
  544.7 120.7 reduce-scatter.25
  672.5 120.9 all-reduce.31
  796.3 23.4 all-reduce.29
  822.5 37.5 reduce-scatter.19
  862.2 38.2 reduce-scatter.15
  902.8 102.1 all-gather.20
  1007.3 100.3 all-gather.18
  1110.1 100.3 all-gather.22
where the time goes:
time: 1230 us
  waiting for transfers between devices  837 us (68%)
  matrix products  124 us (10%)
  local copies, waits for them, and re-layouts  92.5 us (8%)
  blocking collectives  87.9 us (7%)
  other arithmetic  67.7 us (6%)
  between operations  15.3 us (1%)
    reduce_scatter x3, waiting for transfers between devices, sum_rows_over_dp(): lax.psum_scatter(part.astype(jnp.bfloat16), 'dp', scatter_dimension=0, ti...  344 us
    all_gather x3, waiting for transfers between devices, sum_rows_over_dp(): return lax.all_gather(piece, 'dp', axis=0, tiled=True)  242 us
    psum x1, waiting for transfers between devices, per_device(): lax.psum((gain_slot, head_slot, chan_slot, shared_stack), ('dp', 'row', '...  128 us
    unnamed x145, local copies, waits for them, and re-layouts  68.9 us
    unnamed x20, waiting for transfers between devices  56.6 us
    dot_general x3, matrix products, mix_bucket(): within = jnp.einsum('tsh,shp->thp', weights, values, precision=PRECISE)  45.7 us
    psum x1, blocking collectives, per_device(): lax.psum((gain_slot, head_slot, chan_slot, shared_stack), ('dp', 'row', '...  40.3 us
    all_gather x1, blocking collectives, sum_rows_over_dp(): return lax.all_gather(piece, 'dp', axis=0, tiled=True)  33 us
  transfers between devices with their start and end apart: 19, of which 14 were waited for; matrix products, arithmetic and copies ran while one was open for 18% of the time, Pallas kernels for 0%

commit v1 on v0

--- a/solution.py
+++ b/solution.py
@@ -1,3 +1,4 @@
+import functools
 import jax
 import jax.numpy as jnp
 from jax import lax
@@ -8,6 +9,27 @@
 CAP = 256
 EPSILON = 1e-05
 PRECISE = lax.Precision.HIGHEST
+
+
+def begin_face_in(mine, a_name):
+    k_now, everything, state_next = (lax.axis_size(a_name), lax.axis_index(a_name), mine.shape[0])
+    tmp, frame_out = (mine, 1)
+    while frame_out < k_now:
+        tmp = jnp.concatenate(
+            [
+                tmp,
+                lax.ppermute(
+                    tmp, axis_name=a_name, perm=[(w, (w - frame_out) % k_now) for w in range(k_now)]
+                ),
+            ],
+            axis=0,
+        )
+        frame_out = 2 * frame_out
+    block_now = jnp.roll(tmp, shift=everything * state_next, axis=0)
+    return block_now
+
+
+report_area = functools.partial(begin_face_in, a_name="dp")
 
 
 def layout(seq_lengths, seq_owner, bucket, capacity):
@@ -61,7 +83,7 @@
         own = piece.shape[1] - shared_cols
         tail = lax.psum(piece[:, own:].astype(jnp.float32), "col").astype(jnp.bfloat16)
         piece = jnp.concatenate([piece[:, :own], tail], axis=1)
-    return lax.all_gather(piece, "dp", axis=0, tiled=True)
+    return report_area(piece)
 
 
 def mixer_local(

time: 1230 us -> 1550 us (1.26)
  starting transfers between devices: 1.53 us -> 197 us
  other arithmetic: 67.7 us -> 147 us
  waiting for transfers between devices: 837 us -> 881 us
    ppermute x0 -> x12, waiting for transfers between devices: none -> 278 us  [begin_face_in(): lax.ppermute(tmp, axis_name=a_name, perm=[(w, (w - frame_out) % k_now) fo...]
    all_gather x3 -> x0, waiting for transfers between devices: 242 us -> none  [sum_rows_over_dp(): return lax.all_gather(piece, 'dp', axis=0, tiled=True)]
    ppermute x0 -> x12, starting transfers between devices: none -> 196 us  [begin_face_in(): lax.ppermute(tmp, axis_name=a_name, perm=[(w, (w - frame_out) % k_now) fo...]
    another operation x0 -> x2, other arithmetic: none -> 60 us  [per_device(): jnp.stack([gate_total, inner_total], axis=1).astype(jnp.float32)]
    reduce_scatter x3, waiting for transfers between devices: 344 us -> 288 us  [sum_rows_over_dp(): lax.psum_scatter(part.astype(jnp.bfloat16), 'dp', scatter_dimension=0, ti...]
    all_gather x1 -> x0, blocking collectives: 33 us -> none  [sum_rows_over_dp(): return lax.all_gather(piece, 'dp', axis=0, tiled=True)]
    reduce_scatter x1, waiting for transfers between devices: 4.07 us -> 34.1 us  [per_device(): lax.psum_scatter(lax.dot_general(jnp.concatenate([gate_all, inner_all], a...]
    psum x1, waiting for transfers between devices: 128 us -> 149 us  [per_device(): lax.psum((gain_slot, head_slot, chan_slot, shared_stack), ('dp', 'row', '...]
  transfers between devices with their start and end apart: 19 -> 28, of which waited for: 14 -> 17; matrix products, arithmetic and copies ran while one was open for 18% -> 20% of each run, Pallas kernels for 0% -> 0%
where the time goes in v1:
time: 1550 us; the launch traced here: 1540 us
  waiting for transfers between devices  881 us (57%)
  starting transfers between devices  197 us (13%)
  other arithmetic  147 us (9%)
  matrix products  120 us (8%)
  local copies, waits for them, and re-layouts  107 us (7%)
  blocking collectives  75.6 us (5%)
    reduce_scatter x3, waiting for transfers between devices, sum_rows_over_dp(): lax.psum_scatter(part.astype(jnp.bfloat16), 'dp', scatter_dimension=0, ti...  288 us
    ppermute x12, waiting for transfers between devices, begin_face_in(): lax.ppermute(tmp, axis_name=a_name, perm=[(w, (w - frame_out) % k_now) fo...  278 us
    ppermute x12, starting transfers between devices, begin_face_in(): lax.ppermute(tmp, axis_name=a_name, perm=[(w, (w - frame_out) % k_now) fo...  196 us
    psum x1, waiting for transfers between devices, per_device(): lax.psum((gain_slot, head_slot, chan_slot, shared_stack), ('dp', 'row', '...  149 us
    unnamed x190, local copies, waits for them, and re-layouts  80.4 us
    psum x1, blocking collectives, per_device(): lax.psum((gain_slot, head_slot, chan_slot, shared_stack), ('dp', 'row', '...  61.1 us
    another operation x2, other arithmetic, per_device(): jnp.stack([gate_total, inner_total], axis=1).astype(jnp.float32)  60 us
    unnamed x17, waiting for transfers between devices  48.5 us
  transfers between devices with their start and end apart: 28, of which 17 were waited for; matrix products, arithmetic and copies ran while one was open for 20% of the time, Pallas kernels for 0%

profile of v1, /device:TPU:0, one launch (start us, length us, event | category | flops | bytes accessed | tf_op | source)
XLA Modules:
  0.0 1543.0 jit_solution(664375025401396336)
XLA Ops:
  12.9 12.3 copy.71
  25.2 13.7 all-gather.6.cloned.1.call-done
  41.8 12.3 fusion.123
  54.2 10.5 all-gather.10.cloned.1.call-done
  64.7 9.2 fusion.125
  84.7 13.9 reduce-scatter.12.cloned.1.call-done
  110.3 15.8 %fusion.49 = f32[256,40,64]{0,2,1:T(8,128)} fusion(f32[256,40,64]{0,2,1:T(8,128)} %bitcast.90, f32[256,40]{0,1:T(8,128)} %copy-done.38, f32[256,256]{1,0:T(8,128)} %convolution_select_fusion, f32[256,40]{0,1:T(8,128)} %fusion.80, pred[256,256]{1,0:T(8,128)(4,1)S(1)} %fusion.81, f32[256]{0:T(256)S(1)} %copy-done.63, f32[40]{0:T(128)S(1)} %copy-done.80), kind=kOutput, calls=%fused_computation.85 | convolution fusion | flops 2025717760 | bytes 5653664 | tf_op jit(solution)/shard_map/jvp(tsh,shp->thp)/dot_general | solution.py:75
  155.9 17.5 %fusion.24 = (f32[256,40]{0,1:T(8,128)S(1)}, f32[256,40]{0,1:T(8,128)S(1)}, f32[256,40]{0,1:T(8,128)S(1)}, f32[256,256]{1,0:T(8,128)S(1)}) fusion(f32[256,40]{0,1:T(8,128)} %copy-done.38, f32[256,256]{1,0:T(8,128)} %convolution_select_fusion, f32[256,40]{0,1:T(8,128)} %fusion.80, pred[256,256]{1,0:T(8,128)(4,1)S(1)} %fusion.81, ...), kind=kOutput, calls=%fused_computation.48 | convolution fusion | flops 2047903744 | bytes 6038528 | tf_op jit(solution)/shard_map/transpose(jvp(tsh,shp->thp))/dot_general | solution.py:75
  182.0 11.5 bitcast_add_fusion
  228.2 46.9 %reduce-scatter.28.cloned.1.call-done = bf16[160,296]{1,0:T(8,128)(2,1)} async-done(((bf16[1280,296]{1,0:T(8,128)(2,1)}), bf16[160,296]{1,0:T(8,128)(2,1)}) %reduce-scatter.28.cloned.1.call-update) | async-done | bytes 94736
  278.1 8.8 all-gather.14.cloned.1.call-done
  287.0 12.7 fusion.25
  304.6 8.0 convolution_convert_fusion
  323.0 7.9 fusion.124
  331.2 97.4 %reduce-scatter.22.cloned.1.call-done = bf16[160,2560]{1,0:T(8,128)(2,1)} async-done(((bf16[1280,2560]{1,0:T(8,128)(2,1)}), bf16[160,2560]{1,0:T(8,128)(2,1)}) %reduce-scatter.22.cloned.1.call-update) | async-done | bytes 819216 | tf_op jit(solution)/shard_map/reduce_scatter | solution.py:81
  431.2 20.9 %all-reduce.30.cloned.1.call-done = bf16[160,256]{0,1:T(8,128)(2,1)} async-done(((bf16[160,256]{0,1:T(8,128)(2,1)}), bf16[160,256]{0,1:T(8,128)(2,1)}) %all-reduce.30.cloned.1.call-update) | async-done | bytes 81936 | tf_op jit(solution)/shard_map/psum | solution.py:84
  470.3 149.3 %all-reduce.32.cloned.1.call-done = f32[6,2,2560]{2,0,1:T(8,128)} async-done(((f32[6,2,2560]{2,0,1:T(8,128)}), f32[6,2,2560]{2,0,1:T(8,128)}) %all-reduce.32.cloned.1.call-update) | async-done | bytes 122896 | tf_op jit(solution)/shard_map/psum | solution.py:287
  627.4 34.1 %reduce-scatter.20.cloned.1.call-done = f32[256,1280]{1,0:T(8,128)} async-done(((f32[512,1280]{1,0:T(8,128)}), f32[256,1280]{1,0:T(8,128)}) %reduce-scatter.20.cloned.1.call-update) | async-done | bytes 1310736 | tf_op jit(solution)/shard_map/reduce_scatter | solution.py:241
  663.3 123.4 %reduce-scatter.26.cloned.1.call-done = bf16[320,1280]{1,0:T(8,128)(2,1)} async-done(((bf16[2560,1280]{1,0:T(8,128)(2,1)}), bf16[320,1280]{1,0:T(8,128)(2,1)}) %reduce-scatter.26.cloned.1.call-update) | async-done | bytes 819216 | tf_op jit(solution)/shard_map/reduce_scatter | solution.py:81
  789.1 61.1 %all-reduce.26 = (f32[2,1280]{1,0:T(2,128)S(1)}, f32[5,256]{1,0:T(8,128)S(1)}, f32[3,2,40]{2,1,0:T(2,128)S(1)}) all-reduce(f32[2,1280]{1,0:T(2,128)S(1)} %broadcast_multiply_fusion.7, f32[5,256]{1,0:T(8,128)S(1)} %pad_maximum_fusion.14, ...), channel_id=1, replica_groups=mesh['dp'=8,'row'=2,'col'=2] {'dp','row','col'}, use_global_device_ids=true, to_apply=%region_20.21 | all-reduce | flops 4080 | bytes 32640 | tf_op jit(solution)/shard_map/psum | solution.py:287
  854.5 67.4 %reduce-scatter.24.cloned.1.call-done = bf16[160,2560]{1,0:T(8,128)(2,1)} async-done(((bf16[1280,2560]{1,0:T(8,128)(2,1)}), bf16[160,2560]{1,0:T(8,128)(2,1)}) %reduce-scatter.24.cloned.1.call-update) | async-done | bytes 819216 | tf_op jit(solution)/shard_map/reduce_scatter | solution.py:81
  932.2 11.1 collective-permute-done.3
  946.2 14.5 reduce-scatter.16.cloned.1.call-done
  966.4 82.1 %collective-permute-done.10 = bf16[640,1280]{1,0:T(8,128)(2,1)S(1)} collective-permute-done((bf16[640,1280]{1,0:T(8,128)(2,1)}, bf16[640,1280]{1,0:T(8,128)(2,1)S(1)}, u32[]{:S(2)}, u32[]{:S(2)}) %collective-permute-start.10) | collective-permute-done | bytes 1638432 | tf_op jit(solution)/shard_map/ppermute | solution.py:21
  1048.9 70.9 %collective-permute-start.11 = (bf16[1280,1280]{1,0:T(8,128)(2,1)S(1)}, bf16[1280,1280]{1,0:T(8,128)(2,1)S(1)}, u32[]{:S(2)}, u32[]{:S(2)}) collective-permute-start(bf16[1280,1280]{1,0:T(8,128)(2,1)S(1)} %pad_maximum_fusion.2), channel_id=1, source_target_pairs={{0,16},{4,20},{8,24},{12,28},{16,0},{20,4},{24,8},{28,12},{1,17},{... | collective-permute-start | bytes 9830408 | tf_op jit(solution)/shard_map/ppermute | solution.py:21
  1121.4 105.0 %collective-permute-start.5 = (bf16[640,2560]{1,0:T(8,128)(2,1)S(1)}, bf16[640,2560]{1,0:T(8,128)(2,1)S(1)}, u32[]{:S(2)}, u32[]{:S(2)}) collective-permute-start(bf16[640,2560]{1,0:T(8,128)(2,1)S(1)} %pad_maximum_fusion.1), channel_id=1, source_target_pairs={{0,16},{4,20},{8,24},{12,28},{16,0},{20,4},{24,8},{28,12},{1,17},{... | collective-permute-start | bytes 9830408 | tf_op jit(solution)/shard_map/ppermute | solution.py:21
  1227.7 26.8 %fusion.19 = bf16[1280,1,2560]{2,0,1:T(8,128)(2,1)S(1)} fusion(s32[]{:T(128)S(6)} %select_n.129, bf16[160,2560]{1,0:T(8,128)(2,1)S(1)} %copy-done.12, bf16[160,2560]{1,0:T(8,128)(2,1)S(1)} %copy-done.16, bf16[320,2560]{1,0:T(8,128)(2,1)} %collective-permute-done.1, bf16[640,2560]{1,0:T(8,128)(2,1)} %collective-permute-done.2), kind=kLoop, calls=%fused_computation.42 | loop fusion | flops 52428800 | bytes 13107204 | tf_op jit(solution)/shard_map/stack | solution.py:270
  1254.5 179.9 %collective-permute-done.5 = bf16[640,2560]{1,0:T(8,128)(2,1)S(1)} collective-permute-done((bf16[640,2560]{1,0:T(8,128)(2,1)S(1)}, bf16[640,2560]{1,0:T(8,128)(2,1)S(1)}, u32[]{:S(2)}, u32[]{:S(2)}) %collective-permute-start.5) | collective-permute-done | bytes 3276832 | tf_op jit(solution)/shard_map/ppermute | solution.py:21
  1434.4 33.2 %fusion.11 = bf16[1280,1,2560]{2,0,1:T(8,128)(2,1)S(1)} fusion(s32[]{:T(128)S(6)} %select_n.129, bf16[160,2560]{1,0:T(8,128)(2,1)S(1)} %copy-done.14, bf16[160,2560]{1,0:T(8,128)(2,1)S(1)} %copy-done.18, bf16[320,2560]{1,0:T(8,128)(2,1)} %collective-permute-done.4, bf16[640,2560]{1,0:T(8,128)(2,1)S(1)} %collective-permute-done.5), kind=kLoop, calls=%fused_computation.34 | loop fusion | flops 52428800 | bytes 13107204 | tf_op jit(solution)/shard_map/stack | solution.py:270
  1467.6 8.9 maximum_convert_fusion
  1476.6 43.6 %copy.65 = f32[1280,2,2560]{2,1,0:T(2,128)} copy(f32[1280,2,2560]{2,0,1:T(8,128)} %maximum_convert_fusion) | data formatting | bytes 52428800
  1527.1 9.1 dynamic-slice_convert_fusion
  (356 shorter events, 187.9 us)
Async XLA Ops:
  7.2 31.7 %all-gather.6.cloned.1.call-start = ((), (), s32[]{:S(2)}) async-start(), calls=%async_computation.9 | async-start | bytes 1966080 | tf_op jit(solution)/shard_map/all_gather | solution.py:164
  11.8 52.9 %all-gather.10.cloned.1.call-start = ((), (), s32[]{:S(2)}) async-start(), calls=%async_computation.14 | async-start | bytes 1966080 | tf_op jit(solution)/shard_map/all_gather | solution.py:213
  12.6 63.5 %reduce-scatter.14.cloned.1.call-start = ((), (), s32[]{:S(2)}) async-start(), calls=%async_computation.11 | async-start | bytes 909312 | tf_op jit(solution)/shard_map/reduce_scatter | solution.py:173
  41.8 56.8 %reduce-scatter.12.cloned.1.call-start = ((), (), s32[]{:S(2)}) async-start(), calls=%async_computation.10 | async-start | bytes 15728640 | tf_op jit(solution)/shard_map/reduce_scatter | solution.py:167
  54.2 83.5 %reduce-scatter.18.cloned.1.call-start = ((), (), s32[]{:S(2)}) async-start(), calls=%async_computation.15 | async-start | bytes 7864320 | tf_op jit(solution)/shard_map/reduce_scatter | solution.py:215
  74.0 145.5 %all-gather.12.cloned.1.call-start = ((), (), s32[]{:S(2)}) async-start(), calls=%async_computation.16 | async-start | bytes 3932160 | tf_op jit(solution)/shard_map/all_gather | solution.py:232
  181.7 93.4 %reduce-scatter.28.cloned.1.call-start = ((), (), s32[]{:S(2)}) async-start(), calls=%async_computation.24 | async-start | bytes 1105920
  210.3 76.7 %all-gather.14.cloned.1.call-start = ((), (), s32[]{:S(2)}) async-start(), calls=%async_computation.17 | async-start | bytes 3932160 | tf_op jit(solution)/shard_map/all_gather | solution.py:239
  218.7 84.6 %all-gather.8.cloned.1.call-start = ((), (), s32[]{:S(2)}) async-start(), calls=%async_computation.12 | async-start | bytes 3932160 | tf_op jit(solution)/shard_map/all_gather | solution.py:204
  219.5 209.1 %reduce-scatter.22.cloned.1.call-start = ((), (), s32[]{:S(2)}) async-start(), calls=%async_computation.19 | async-start | bytes 7372800 | tf_op jit(solution)/shard_map/reduce_scatter | solution.py:81
  227.3 224.8 %all-reduce.30.cloned.1.call-start = ((), (), s32[]{:S(2)}) async-start(), calls=%async_computation.21 | async-start | bytes 262144 | tf_op jit(solution)/shard_map/psum | solution.py:84
  276.8 342.7 %all-reduce.32.cloned.1.call-start = ((), (), s32[]{:S(2)}) async-start(), calls=%async_computation.23 | async-start | bytes 327680 | tf_op jit(solution)/shard_map/psum | solution.py:287
  277.7 383.8 %reduce-scatter.20.cloned.1.call-start = ((), (), s32[]{:S(2)}) async-start(), calls=%async_computation.18 | async-start | bytes 3932160 | tf_op jit(solution)/shard_map/reduce_scatter | solution.py:241
  303.3 483.4 %reduce-scatter.26.cloned.1.call-start = ((), (), s32[]{:S(2)}) async-start(), calls=%async_computation.22 | async-start | bytes 7372800 | tf_op jit(solution)/shard_map/reduce_scatter | solution.py:81
  312.6 609.2 %reduce-scatter.24.cloned.1.call-start = ((), (), s32[]{:S(2)}) async-start(), calls=%async_computation.20 | async-start | bytes 7372800 | tf_op jit(solution)/shard_map/reduce_scatter | solution.py:81
  321.3 639.3 %reduce-scatter.16.cloned.1.call-start = ((), (), s32[]{:S(2)}) async-start(), calls=%async_computation.13 | async-start | bytes 3932160 | tf_op jit(solution)/shard_map/reduce_scatter | solution.py:206
  331.1 139.1 %copy-start.70 = (f32[256]{0:T(256)S(1)}, f32[256]{0:T(256)}, u32[]{:S(2)}) copy-start(f32[256]{0:T(256)} %get-tuple-element.87) | copy-start | bytes 3076
  428.6 34.2 %collective-permute-start = (bf16[160,2560]{1,0:T(8,128)(2,1)}, bf16[160,2560]{1,0:T(8,128)(2,1)S(1)}, u32[]{:S(2)}, u32[]{:S(2)}) collective-permute-start(bf16[160,2560]{1,0:T(8,128)(2,1)} %reduce-scatter.22.cloned.1.call-done), channel_id=1, source_target_pairs={{0,28},{4,0},{8,4},{12,8},{16,12},{20,16},{24,20},{28,24},{1,29},{... | collective-permute-start | bytes 2457608 | tf_op jit(solution)/shard_map/ppermute | solution.py:21
  453.1 7.0 collective-permute-start.6
  461.2 7.4 collective-permute-start.7
  462.8 162.0 %copy-start.15 = (bf16[160,2560]{1,0:T(8,128)(2,1)}, bf16[160,2560]{1,0:T(8,128)(2,1)S(1)}, u32[]{:S(2)}) copy-start(bf16[160,2560]{1,0:T(8,128)(2,1)S(1)} %collective-permute-done) | copy-start | bytes 2457604
  465.5 458.7 %collective-permute-start.1 = (bf16[320,2560]{1,0:T(8,128)(2,1)}, bf16[320,2560]{1,0:T(8,128)(2,1)}, u32[]{:S(2)}, u32[]{:S(2)}) collective-permute-start(bf16[320,2560]{1,0:T(8,128)(2,1)} %pad_maximum_fusion.3), channel_id=1, source_target_pairs={{0,24},{4,28},{8,0},{12,4},{16,8},{20,12},{24,16},{28,20},{1,25},{... | collective-permute-start | bytes 4915208 | tf_op jit(solution)/shard_map/ppermute | solution.py:21
  468.8 153.9 %collective-permute-start.8 = (bf16[640,296]{0,1:T(8,128)(2,1)S(1)}, bf16[640,296]{0,1:T(8,128)(2,1)S(1)}, u32[]{:S(2)}, u32[]{:S(2)}) collective-permute-start(bf16[640,296]{0,1:T(8,128)(2,1)S(1)} %pad_maximum_fusion.10), channel_id=1, source_target_pairs={{0,16},{4,20},{8,24},{12,28},{16,0},{20,4},{24,8},{28,12},{1,17},{... | collective-permute-start | bytes 1136648 | tf_op jit(solution)/shard_map/ppermute | solution.py:21
  786.7 141.4 %collective-permute-start.9 = (bf16[320,1280]{1,0:T(8,128)(2,1)}, bf16[320,1280]{1,0:T(8,128)(2,1)S(1)}, u32[]{:S(2)}, u32[]{:S(2)}) collective-permute-start(bf16[320,1280]{1,0:T(8,128)(2,1)} %reduce-scatter.26.cloned.1.call-done), channel_id=1, source_target_pairs={{0,28},{4,0},{8,4},{12,8},{16,12},{20,16},{24,20},{28,24},{1,29},{... | collective-permute-start | bytes 2457608 | tf_op jit(solution)/shard_map/ppermute | solution.py:21
  921.8 21.4 %collective-permute-start.3 = (bf16[160,2560]{1,0:T(8,128)(2,1)}, bf16[160,2560]{1,0:T(8,128)(2,1)S(1)}, u32[]{:S(2)}, u32[]{:S(2)}) collective-permute-start(bf16[160,2560]{1,0:T(8,128)(2,1)} %reduce-scatter.24.cloned.1.call-done), channel_id=1, source_target_pairs={{0,28},{4,0},{8,4},{12,8},{16,12},{20,16},{24,20},{28,24},{1,29},{... | collective-permute-start | bytes 2457608 | tf_op jit(solution)/shard_map/ppermute | solution.py:21
  927.4 300.3 %collective-permute-start.2 = (bf16[640,2560]{1,0:T(8,128)(2,1)}, bf16[640,2560]{1,0:T(8,128)(2,1)}, u32[]{:S(2)}, u32[]{:S(2)}) collective-permute-start(bf16[640,2560]{1,0:T(8,128)(2,1)} %pad_maximum_fusion), channel_id=1, source_target_pairs={{0,16},{4,20},{8,24},{12,28},{16,0},{20,4},{24,8},{28,12},{1,17},{... | collective-permute-start | bytes 9830408 | tf_op jit(solution)/shard_map/ppermute | solution.py:21
  929.4 119.2 %collective-permute-start.10 = (bf16[640,1280]{1,0:T(8,128)(2,1)}, bf16[640,1280]{1,0:T(8,128)(2,1)S(1)}, u32[]{:S(2)}, u32[]{:S(2)}) collective-permute-start(bf16[640,1280]{1,0:T(8,128)(2,1)} %pad_maximum_fusion.5), channel_id=1, source_target_pairs={{0,24},{4,28},{8,0},{12,4},{16,8},{20,12},{24,16},{28,20},{1,25},{... | collective-permute-start | bytes 4915208 | tf_op jit(solution)/shard_map/ppermute | solution.py:21
  944.7 175.1 %collective-permute-start.4 = (bf16[320,2560]{1,0:T(8,128)(2,1)}, bf16[320,2560]{1,0:T(8,128)(2,1)}, u32[]{:S(2)}, u32[]{:S(2)}) collective-permute-start(bf16[320,2560]{1,0:T(8,128)(2,1)} %pad_maximum_fusion.4), channel_id=1, source_target_pairs={{0,24},{4,28},{8,0},{12,4},{16,8},{20,12},{24,16},{28,20},{1,25},{... | collective-permute-start | bytes 4915208 | tf_op jit(solution)/shard_map/ppermute | solution.py:21
  966.4 153.4 %copy-start.14 = (bf16[160,2560]{1,0:T(8,128)(2,1)S(1)}, bf16[160,2560]{1,0:T(8,128)(2,1)}, u32[]{:S(2)}) copy-start(bf16[160,2560]{1,0:T(8,128)(2,1)} %reduce-scatter.24.cloned.1.call-done) | copy-start | bytes 2457604
  966.4 153.4 %copy-start.18 = (bf16[160,2560]{1,0:T(8,128)(2,1)S(1)}, bf16[160,2560]{1,0:T(8,128)(2,1)}, u32[]{:S(2)}) copy-start(bf16[160,2560]{1,0:T(8,128)(2,1)} %copy-done.17) | copy-start | bytes 2457604
  1048.9 471.3 %collective-permute-start.11 = (bf16[1280,1280]{1,0:T(8,128)(2,1)S(1)}, bf16[1280,1280]{1,0:T(8,128)(2,1)S(1)}, u32[]{:S(2)}, u32[]{:S(2)}) collective-permute-start(bf16[1280,1280]{1,0:T(8,128)(2,1)S(1)} %pad_maximum_fusion.2), channel_id=1, source_target_pairs={{0,16},{4,20},{8,24},{12,28},{16,0},{20,4},{24,8},{28,12},{1,17},{... | collective-permute-start | bytes 9830408 | tf_op jit(solution)/shard_map/ppermute | solution.py:21
  1121.4 313.1 %collective-permute-start.5 = (bf16[640,2560]{1,0:T(8,128)(2,1)S(1)}, bf16[640,2560]{1,0:T(8,128)(2,1)S(1)}, u32[]{:S(2)}, u32[]{:S(2)}) collective-permute-start(bf16[640,2560]{1,0:T(8,128)(2,1)S(1)} %pad_maximum_fusion.1), channel_id=1, source_target_pairs={{0,16},{4,20},{8,24},{12,28},{16,0},{20,4},{24,8},{28,12},{1,17},{... | collective-permute-start | bytes 9830408 | tf_op jit(solution)/shard_map/ppermute | solution.py:21
  (87 other events, 1886.0 us)
Sparse Core Ops, SparseCore 0:
  11.9 26.9 all-gather.5
  40.4 24.2 all-gather.9
  67.6 8.0 reduce-scatter.13
  78.4 20.1 reduce-scatter.11
  100.8 14.4 reduce-scatter.17
  181.8 12.5 all-gather.11
  210.4 64.6 reduce-scatter.27
  276.6 10.3 all-gather.13
  289.1 12.5 all-gather.7
  305.7 122.8 reduce-scatter.21
  431.5 20.5 all-reduce.29
  459.0 160.4 all-reduce.31
  621.9 39.5 reduce-scatter.19
  665.0 121.6 reduce-scatter.25
  791.1 130.6 reduce-scatter.23
  923.9 36.6 reduce-scatter.15
